TPU v7x, 32 devices: a whole 2x2x4 slice. The times are simulated.
32 devices in a mesh: groups: 2 (over x), wide: 16 (over z, y, core).
Axes of the slice: x: 2, y: 2, z: 4, core: 2. Of those that a mesh axis runs over, the one named last changes fastest.
Arguments:
- embeds: bfloat16 [32768, 768], P(('groups', 'wide')), parts along dimension 0
- labels: int32 [32768], P(('groups', 'wide')), parts along dimension 0, may hold values from 0 to 63, as said below
Outputs:
- average: bfloat16 [32768, 768], P(('groups', 'wide')), parts along dimension 0
- density: bfloat16 [32768], P(('groups', 'wide')), parts along dimension 0
There are 2 independent parts, one for each index of `groups`. A program takes and returns all parts, laid end to end along the dimension named above; each array names one. Nothing has to cross between parts.
Inputs may be any that keep to these rules, and one draw needn't show every extreme that they name: `labels`: cluster c is local cluster c % 4 of owner c // 4. Of the rows of one device, at most 128 have clusters of one owner, and on every device some owner gets exactly 128.
All inputs are finite; a program needn't handle non-finite values.
Results may differ from a plain program's by a relative error of at most 0.0034.
Values may be sent and summed in bfloat16 or wider, within the bound.
A program may use at most 64 MiB of HBM per device.

v0:
```python
import jax
import jax.numpy as jnp
from jax import lax
from jax.sharding import PartitionSpec as P

CL_DEV = 4


TAU = 0.2


def tile_terms(query, qtag, keys, ktag):
    sim = jnp.dot(query, keys.T, preferred_element_type=jnp.float32)
    same = (qtag[:, None] == ktag[None, :]) & (ktag[None, :] > 0)
    weight = jnp.where(same, jnp.exp((sim - 1.0) / TAU), 0.0)
    numer = jnp.dot(weight.astype(jnp.bfloat16), keys, preferred_element_type=jnp.float32)
    return (jnp.sum(weight, axis=1), numer)


def finish(dens, numer, qtag):
    dens = jnp.where(qtag > 0, dens, 1.0)
    return ((numer / dens[:, None]).astype(jnp.bfloat16), dens.astype(jnp.bfloat16))


def per_device(embeds, labels):
    rows_dev, width = embeds.shape
    n_wide = lax.axis_size("wide")
    capacity = 2 * rows_dev // n_wide
    slots_all = n_wide * capacity
    values = embeds.astype(jnp.float32)
    squared = jnp.sum(values * values, axis=1, keepdims=True)
    inside = squared + 1e-06
    unit = (values * lax.rsqrt(inside)).astype(jnp.bfloat16)
    dest = labels // CL_DEV
    local = labels % CL_DEV
    onehot = (dest[:, None] == jnp.arange(n_wide, dtype=jnp.int32)[None, :]).astype(jnp.int32)
    running = jnp.cumsum(onehot, axis=0) - 1
    rank = jnp.sum(jnp.where(onehot > 0, running, 0), axis=1)
    position = dest * capacity + rank
    outgoing = jnp.zeros((slots_all, width), jnp.bfloat16).at[position].set(unit)
    out_tags = (
        jnp.zeros((slots_all,), jnp.bfloat16).at[position].set((local + 1).astype(jnp.bfloat16))
    )
    received, in_tags = (
        lax.all_to_all(outgoing, "wide", split_axis=0, concat_axis=0, tiled=True),
        lax.all_to_all(out_tags, "wide", split_axis=0, concat_axis=0, tiled=True),
    )
    tag = in_tags.astype(jnp.int32)
    blk = min(512, slots_all)
    n_tiles = slots_all // blk

    def per_block(item):
        query, qtag = item
        dens, numer = tile_terms(query, qtag, received, tag)
        return finish(dens, numer, qtag)

    avg_tiles, dens_tiles = lax.map(
        per_block, (received.reshape(n_tiles, blk, width), tag.reshape(n_tiles, blk))
    )
    averaged = avg_tiles.reshape(slots_all, width)
    densities = dens_tiles.reshape(slots_all)
    back_avg, back_dens = (
        lax.all_to_all(averaged, "wide", split_axis=0, concat_axis=0, tiled=True),
        lax.all_to_all(densities, "wide", split_axis=0, concat_axis=0, tiled=True),
    )
    return (back_avg[position], back_dens[position])


def solution(mesh):
    placed = (P(("groups", "wide"), None), P(("groups", "wide")))
    return jax.shard_map(
        per_device,
        mesh=mesh,
        in_specs=placed,
        out_specs=(P(("groups", "wide"), None), P(("groups", "wide"))),
        check_vma=False,
    )
```

profile of v0, /device:TPU:15, one launch (start us, length us, event | category | flops | bytes accessed | tf_op | source)
XLA Modules:
  0.0 229.3 jit_solution(2084355715589637510)
XLA Ops:
  0.6 0.0 copy-start
  0.6 0.8 fusion.24
  1.5 4.5 %reduce-window.6 = s32[16,8,128]{2,1,0:T(8,128)S(1)} reduce-window(s32[16,8,128]{2,1,0:T(8,128)S(1)} %fusion.22, s32[]{:T(128)} %constant.83.clone.1), window={size=1x1x128 pad=0_0x0_0x127_0}, to_apply=%region_0.0 | reduce-window | flops 2080768 | bytes 131076 | tf_op jit(solution)/shard_map/reduce-window
  6.0 0.1 slice.12
  6.1 0.1 copy.10
  6.2 0.1 copy.11
  6.3 0.1 add_add_fusion
  6.5 7.6 %scatter_custom_fusion = bf16[2048]{0:T(1024)(128)(2,1)S(1)} fusion(s32[1024]{0:T(1024)S(1)} %get-tuple-element.109, bf16[1024]{0:T(1024)(128)(2,1)S(1)} %get-tuple-element.112, bf16[]{:T(256)} %constant.84.clone.1), kind=kCustom, calls=%fused_computation.46 | custom fusion | bytes 4098 | tf_op jit(solution)/shard_map/scatter | solution.py:42
  14.1 0.6 copy.12
  14.7 6.6 %all-to-all-start = ((bf16[16,128,1]{1,2,0:T(2,128)(2,1)}), bf16[16,128,1]{1,2,0:T(2,128)(2,1)S(1)}, u32[]{:S(2)}, u32[]{:S(2)}) async-start(bf16[16,128,1]{1,2,0:T(2,128)(2,1)} %copy.12), calls=%async_computation | async-start | bytes 16384 | tf_op jit(solution)/shard_map/all_to_all | solution.py:46
  21.2 1.8 fusion.14
  23.0 0.0 copy-done
  23.0 7.8 %scatter_custom_fusion.1 = bf16[2048,768]{1,0:T(8,128)(2,1)} fusion(s32[1024]{0:T(1024)S(1)} %get-tuple-element.109, bf16[1024,768]{1,0:T(8,128)(2,1)S(1)} %copy-done, f32[1024]{0:T(1024)S(1)} %add_rsqrt_fusion, bf16[]{:T(256)} %constant.84.clone.1), kind=kCustom, calls=%fused_computation.22 | custom fusion | flops 2359296 | bytes 4722690 | tf_op jit(solution)/shard_map/scatter | solution.py:40
  30.8 0.0 all-to-all-done
  30.8 6.0 %all-to-all-start.1 = ((bf16[16,128,768]{2,1,0:T(8,128)(2,1)}), bf16[16,128,768]{2,1,0:T(8,128)(2,1)S(1)}, u32[]{:S(2)}, u32[]{:S(2)}) async-start(bf16[16,128,768]{2,1,0:T(8,128)(2,1)} %bitcast.9), calls=%async_computation.1 | async-start | bytes 6291456 | tf_op jit(solution)/shard_map/all_to_all | solution.py:45
  36.9 69.8 %all-to-all-done.1 = bf16[16,128,768]{2,1,0:T(8,128)(2,1)S(1)} async-done(((bf16[16,128,768]{2,1,0:T(8,128)(2,1)}), bf16[16,128,768]{2,1,0:T(8,128)(2,1)S(1)}, u32[]{:S(2)}, u32[]{:S(2)}) %all-to-all-start.1) | async-done | bytes 3145760 | tf_op jit(solution)/shard_map/all_to_all | solution.py:45
  106.7 32.7 %while.14 = (s32[]{:T(128)}, bf16[4,512,768]{2,1,0:T(8,128)(2,1)}, bf16[4,512]{1,0:T(4,128)(2,1)S(1)}, s32[4,512]{1,0:T(4,128)S(1)}, s32[2048]{0:T(1024)S(1)}, /...) while((s32[]{:T(128)}, bf16[4,512,768]{2,1,0:T(8,128)(2,1)}, ...), condition=%wide.region_8.9_spmd, body=%wide.region_6.8_spmd.sunk | while | flops 3229355520 | bytes 12102777 | solution.py:57
  106.7 3.8 %fusion.42 = (f32[512]{0:T(512)S(1)}, bf16[512,2048]{1,0:T(8,128)(2,1)}) fusion(bf16[2048,768]{1,0:T(8,128)(2,1)S(1)} %get-tuple-element.187, bf16[4,512,768]{2,1,0:T(8,128)(2,1)S(1)} %bitcast.57, s32[]{:T(128)S(6)} %copy.21, pred[2048]{0:T(1024)(128)(4,1)S(1)} %broadcast_compare_fusion.2, s32[2048]{0:T(1024)S(1)} %get-tuple-element.185, ...), kind=kOutput, calls=%fused_computation.49.clone.1 | convolution fusion | flops 1617952256 | bytes 6043652 | tf_op jit(solution)/shard_map/while/body/eval_jaxpr/dot_general | solution.py:13
  110.6 4.3 %fusion.43 = bf16[4,512,768]{2,1,0:T(8,128)(2,1)} fusion(bf16[4,512,768]{2,1,0:T(8,128)(2,1)} %get-tuple-element.173, s32[]{:T(128)S(6)} %copy.21, bf16[2048,768]{1,0:T(8,128)(2,1)S(1)} %get-tuple-element.187, bf16[512,2048]{1,0:T(8,128)(2,1)} %get-tuple-element.161, f32[512]{0:T(512)S(1)} %compare_select_fusion.5), kind=kOutput, calls=%fused_computation.9.clone.1 | convolution fusion | flops 1611399168 | bytes 6031364 | tf_op jit(solution)/shard_map/while/body/eval_jaxpr/dot_general | solution.py:16
  114.9 3.8 %fusion.42 = (f32[512]{0:T(512)S(1)}, bf16[512,2048]{1,0:T(8,128)(2,1)}) fusion(bf16[2048,768]{1,0:T(8,128)(2,1)S(1)} %get-tuple-element.187, bf16[4,512,768]{2,1,0:T(8,128)(2,1)S(1)} %bitcast.57, s32[]{:T(128)S(6)} %copy.21, pred[2048]{0:T(1024)(128)(4,1)S(1)} %broadcast_compare_fusion.2, s32[2048]{0:T(1024)S(1)} %get-tuple-element.185, ...), kind=kOutput, calls=%fused_computation.49.clone.1 | convolution fusion | flops 1617952256 | bytes 6043652 | tf_op jit(solution)/shard_map/while/body/eval_jaxpr/dot_general | solution.py:13
  118.7 4.3 %fusion.43 = bf16[4,512,768]{2,1,0:T(8,128)(2,1)} fusion(bf16[4,512,768]{2,1,0:T(8,128)(2,1)} %get-tuple-element.173, s32[]{:T(128)S(6)} %copy.21, bf16[2048,768]{1,0:T(8,128)(2,1)S(1)} %get-tuple-element.187, bf16[512,2048]{1,0:T(8,128)(2,1)} %get-tuple-element.161, f32[512]{0:T(512)S(1)} %compare_select_fusion.5), kind=kOutput, calls=%fused_computation.9.clone.1 | convolution fusion | flops 1611399168 | bytes 6031364 | tf_op jit(solution)/shard_map/while/body/eval_jaxpr/dot_general | solution.py:16
  123.1 3.8 %fusion.42 = (f32[512]{0:T(512)S(1)}, bf16[512,2048]{1,0:T(8,128)(2,1)}) fusion(bf16[2048,768]{1,0:T(8,128)(2,1)S(1)} %get-tuple-element.187, bf16[4,512,768]{2,1,0:T(8,128)(2,1)S(1)} %bitcast.57, s32[]{:T(128)S(6)} %copy.21, pred[2048]{0:T(1024)(128)(4,1)S(1)} %broadcast_compare_fusion.2, s32[2048]{0:T(1024)S(1)} %get-tuple-element.185, ...), kind=kOutput, calls=%fused_computation.49.clone.1 | convolution fusion | flops 1617952256 | bytes 6043652 | tf_op jit(solution)/shard_map/while/body/eval_jaxpr/dot_general | solution.py:13
  126.9 4.3 %fusion.43 = bf16[4,512,768]{2,1,0:T(8,128)(2,1)} fusion(bf16[4,512,768]{2,1,0:T(8,128)(2,1)} %get-tuple-element.173, s32[]{:T(128)S(6)} %copy.21, bf16[2048,768]{1,0:T(8,128)(2,1)S(1)} %get-tuple-element.187, bf16[512,2048]{1,0:T(8,128)(2,1)} %get-tuple-element.161, f32[512]{0:T(512)S(1)} %compare_select_fusion.5), kind=kOutput, calls=%fused_computation.9.clone.1 | convolution fusion | flops 1611399168 | bytes 6031364 | tf_op jit(solution)/shard_map/while/body/eval_jaxpr/dot_general | solution.py:16
  131.2 3.8 %fusion.42 = (f32[512]{0:T(512)S(1)}, bf16[512,2048]{1,0:T(8,128)(2,1)}) fusion(bf16[2048,768]{1,0:T(8,128)(2,1)S(1)} %get-tuple-element.187, bf16[4,512,768]{2,1,0:T(8,128)(2,1)S(1)} %bitcast.57, s32[]{:T(128)S(6)} %copy.21, pred[2048]{0:T(1024)(128)(4,1)S(1)} %broadcast_compare_fusion.2, s32[2048]{0:T(1024)S(1)} %get-tuple-element.185, ...), kind=kOutput, calls=%fused_computation.49.clone.1 | convolution fusion | flops 1617952256 | bytes 6043652 | tf_op jit(solution)/shard_map/while/body/eval_jaxpr/dot_general | solution.py:13
  135.1 4.3 %fusion.43 = bf16[4,512,768]{2,1,0:T(8,128)(2,1)} fusion(bf16[4,512,768]{2,1,0:T(8,128)(2,1)} %get-tuple-element.173, s32[]{:T(128)S(6)} %copy.21, bf16[2048,768]{1,0:T(8,128)(2,1)S(1)} %get-tuple-element.187, bf16[512,2048]{1,0:T(8,128)(2,1)} %get-tuple-element.161, f32[512]{0:T(512)S(1)} %compare_select_fusion.5), kind=kOutput, calls=%fused_computation.9.clone.1 | convolution fusion | flops 1611399168 | bytes 6031364 | tf_op jit(solution)/shard_map/while/body/eval_jaxpr/dot_general | solution.py:16
  139.4 8.5 %all_to_all.46 = bf16[16,128,1]{1,2,0:T(2,128)(2,1)S(1)} all-to-all(bf16[16,128,1]{1,2,0:T(2,128)(2,1)S(1)} %all_to_all.41), channel_id=1, replica_groups=mesh['groups'=2,'wide'=16] {'wide'}, dimensions={0} | all-to-all | bytes 8192 | tf_op jit(solution)/shard_map/all_to_all | solution.py:64
  147.9 6.3 %all-to-all-start.2 = ((bf16[16,128,768]{2,1,0:T(8,128)(2,1)}), bf16[16,128,768]{2,1,0:T(8,128)(2,1)S(1)}, u32[]{:S(2)}, u32[]{:S(2)}) async-start(bf16[16,128,768]{2,1,0:T(8,128)(2,1)} %bitcast.59), calls=%async_computation.2 | async-start | bytes 6291456 | tf_op jit(solution)/shard_map/all_to_all | solution.py:63
  154.2 11.3 %gather_fusion.1 = bf16[1024]{0:T(1024)(128)(2,1)} fusion(bf16[2048]{0:T(1024)(128)(2,1)S(1)} %bitcast.53, s32[1024]{0:T(1024)S(1)} %get-tuple-element.108), kind=kCustom, calls=%fused_computation.1 | custom fusion | bytes 8192 | tf_op jit(solution)/shard_map/gather | solution.py:66
  165.5 58.6 %all-to-all-done.2 = bf16[16,128,768]{2,1,0:T(8,128)(2,1)S(1)} async-done(((bf16[16,128,768]{2,1,0:T(8,128)(2,1)}), bf16[16,128,768]{2,1,0:T(8,128)(2,1)S(1)}, u32[]{:S(2)}, u32[]{:S(2)}) %all-to-all-start.2) | async-done | bytes 3145760 | tf_op jit(solution)/shard_map/all_to_all | solution.py:63
  224.1 5.2 %gather_fusion = bf16[1024,768]{1,0:T(8,128)(2,1)} fusion(bf16[2048,768]{1,0:T(8,128)(2,1)S(1)} %bitcast.54, s32[1024]{0:T(1024)S(1)} %get-tuple-element.108), kind=kCustom, calls=%fused_computation | custom fusion | bytes 3149824 | tf_op jit(solution)/shard_map/gather | solution.py:66
  (33 shorter events, 0.5 us)
Async XLA Ops:
  0.6 22.4 %copy-start = (bf16[1024,768]{1,0:T(8,128)(2,1)S(1)}, bf16[1024,768]{1,0:T(8,128)(2,1)}, u32[]{:S(2)}) copy-start(bf16[1024,768]{1,0:T(8,128)(2,1)} %param.4) | copy-start | bytes 4718596
  14.7 16.1 %all-to-all-start = ((bf16[16,128,1]{1,2,0:T(2,128)(2,1)}), bf16[16,128,1]{1,2,0:T(2,128)(2,1)S(1)}, u32[]{:S(2)}, u32[]{:S(2)}) async-start(bf16[16,128,1]{1,2,0:T(2,128)(2,1)} %copy.12), calls=%async_computation | async-start | bytes 16384 | tf_op jit(solution)/shard_map/all_to_all | solution.py:46
  30.8 75.9 %all-to-all-start.1 = ((bf16[16,128,768]{2,1,0:T(8,128)(2,1)}), bf16[16,128,768]{2,1,0:T(8,128)(2,1)S(1)}, u32[]{:S(2)}, u32[]{:S(2)}) async-start(bf16[16,128,768]{2,1,0:T(8,128)(2,1)} %bitcast.9), calls=%async_computation.1 | async-start | bytes 6291456 | tf_op jit(solution)/shard_map/all_to_all | solution.py:45
  147.9 76.2 %all-to-all-start.2 = ((bf16[16,128,768]{2,1,0:T(8,128)(2,1)}), bf16[16,128,768]{2,1,0:T(8,128)(2,1)S(1)}, u32[]{:S(2)}, u32[]{:S(2)}) async-start(bf16[16,128,768]{2,1,0:T(8,128)(2,1)} %bitcast.59), calls=%async_computation.2 | async-start | bytes 6291456 | tf_op jit(solution)/shard_map/all_to_all | solution.py:63
where the time goes:
time: 230 us; the launch traced here: 229 us
  waiting for transfers between devices  128 us (56%)
  matrix products  32.4 us (14%)
  local copies, waits for them, and re-layouts  25.2 us (11%)
  starting transfers between devices  18.8 us (8%)
  other arithmetic  15.2 us (7%)
  blocking collectives  8.5 us (4%)
    all_to_all x1, waiting for transfers between devices, per_device(): lax.all_to_all(outgoing, 'wide', split_axis=0, concat_axis=0, tiled=True)  69.8 us
    all_to_all x1, waiting for transfers between devices, per_device(): lax.all_to_all(averaged, 'wide', split_axis=0, concat_axis=0, tiled=True)  58.6 us
    dot_general x4, matrix products, tile_terms(): jnp.dot(weight.astype(jnp.bfloat16), keys, preferred_element_type=jnp.flo...  17.3 us
    gather x2, local copies, waits for them, and re-layouts, per_device(): return (back_avg[position], back_dens[position])  16.5 us
    dot_general x4, matrix products, tile_terms(): sim = jnp.dot(query, keys.T, preferred_element_type=jnp.float32)  15.1 us
    all_to_all x1, blocking collectives, per_device(): lax.all_to_all(densities, 'wide', split_axis=0, concat_axis=0, tiled=True)  8.5 us
    scatter x1, other arithmetic, per_device(): jnp.zeros((slots_all, width), jnp.bfloat16).at[position].set(unit)  7.76 us
    scatter x1, local copies, waits for them, and re-layouts, per_device(): jnp.zeros((slots_all,), jnp.bfloat16).at[position]  7.59 us
  transfers between devices with their start and end apart: 3, of which 2 were waited for; matrix products, arithmetic and copies ran while one was open for 9% of the time, Pallas kernels for 0%

commit v1 on v0

v1 whole, which is shorter than its diff:
```python
import functools
import math

import jax
import jax.numpy as jnp
from jax import lax
from jax.experimental import pallas as pl
from jax.experimental.pallas import tpu as pltpu
from jax.sharding import PartitionSpec as P

CL_DEV = 4
TAU = 0.2
SCALE = math.log2(math.e) / TAU
TILE = 256
F32 = jnp.float32
BF16 = jnp.bfloat16


def kernel(n, embeds, labels, out, out_dens,
           unit, send, recv, back, home, numer, total,
           stag, rtag, bden, hden, ktag, qtag, dacc, pos, pos_t,
           s_rows, r_rows, s_tags, r_tags, s_back, r_back, s_den, r_den):
    rows, width = embeds.shape
    cap = 2 * rows // n
    slots = n * cap
    tiles = slots // TILE
    per_tile = TILE // cap
    per_lane = 128 // cap
    me = lax.axis_index("wide")

    barrier = pltpu.get_barrier_semaphore()

    @pl.loop(1, n)
    def _(k):
        pl.semaphore_signal(barrier, inc=1, device_id={"wide": lax.rem(me + k, n)},
                            device_id_type=pl.DeviceIdType.MESH)

    def to_dest(k):
        return {"wide": lax.rem(me + k, n)}

    def to_source(k):
        return {"wide": lax.rem(me - k + n, n)}

    def slot_rows(k):
        return pl.ds(pl.multiple_of(k * cap, cap), cap)

    def slot_tags(k):
        return pl.ds(pl.multiple_of(k * 8, 8), 8)

    def remote(src, dst, ssem, rsem, where):
        return pltpu.make_async_remote_copy(
            src_ref=src, dst_ref=dst, send_sem=ssem, recv_sem=rsem,
            device_id=where, device_id_type=pl.DeviceIdType.MESH)

    def go_rows(k):
        return remote(send.at[slot_rows(k)], recv.at[slot_rows(k)], s_rows.at[k], r_rows.at[k], to_dest(k))

    def go_tags(k):
        return remote(stag.at[slot_tags(k)], rtag.at[slot_tags(k)], s_tags.at[k], r_tags.at[k], to_dest(k))

    def back_rows(k):
        return remote(back.at[slot_rows(k)], home.at[slot_rows(k)], s_back.at[k], r_back.at[k], to_source(k))

    def back_dens(k):
        return remote(bden.at[slot_tags(k)], hden.at[slot_tags(k)], s_den.at[k], r_den.at[k], to_source(k))

    def tile_of(t):
        return pl.ds(pl.multiple_of(t * TILE, TILE), TILE)

    @pl.loop(0, rows // 128)
    def _(b):
        at = pl.ds(pl.multiple_of(b * 128, 128), 128)
        x = embeds[at, :].astype(F32)
        inside = jnp.sum(x * x, axis=1, keepdims=True) + 1e-06
        unit[at, :] = (x * lax.rsqrt(inside)).astype(BF16)

    lab = labels[...]
    ahead = (lab >> 2) - me
    ahead = jnp.where(ahead < 0, ahead + n, ahead)
    tag = ((lab & 3) + 1).astype(F32)
    which = lax.broadcasted_iota(jnp.int32, (n, TILE), 0)
    before = (lax.broadcasted_iota(jnp.int32, (TILE, TILE), 0)
              < lax.broadcasted_iota(jnp.int32, (TILE, TILE), 1)).astype(F32).astype(BF16)
    running = jnp.zeros((n, 1), F32)
    for b in range(rows // TILE):
        piece = ahead[:, b * TILE:(b + 1) * TILE]
        hot = (jnp.broadcast_to(piece, (n, TILE)) == which).astype(F32)
        rank = jnp.dot(hot.astype(BF16), before, preferred_element_type=F32) + running
        running = running + jnp.sum(hot, axis=1, keepdims=True)
        rank = jnp.sum(hot * rank, axis=0, keepdims=True)
        pos[:, b * TILE:(b + 1) * TILE] = jnp.broadcast_to(
            rank + (piece * cap).astype(F32), (8, TILE))

    tag8 = jnp.broadcast_to(tag, (8, rows)).astype(BF16)
    lane = lax.broadcasted_iota(jnp.int32, (8, 128), 1)

    def picks(t):
        ids = (lax.broadcasted_iota(jnp.int32, (TILE, rows), 0) + t * TILE).astype(F32)
        return jnp.where(ids == pos[0:1, :], 1.0, 0.0).astype(BF16)

    def own_lanes(piece, j):
        if per_lane == 1:
            return piece
        low = (j % per_lane) * cap
        return jnp.where((lane >= low) & (lane < low + cap), piece, 0.0)

    def pack(t):
        sel = picks(t)
        send[tile_of(t), :] = jnp.dot(sel, unit[...], preferred_element_type=F32).astype(BF16)
        tags = lax.dot_general(tag8, sel, (((1,), (1,)), ((), ())), preferred_element_type=F32)
        for j in range(per_tile):
            at = j // per_lane * 128
            stag[slot_tags(t * per_tile + j), :] = own_lanes(tags[:, at:at + 128], j)

    def launch(t, first):
        for j in range(first, per_tile):
            go_rows(t * per_tile + j).start()
            go_tags(t * per_tile + j).start()

    pack(0)
    pl.semaphore_wait(barrier, n - 1)
    launch(0, 1)
    recv[0:cap, :] = send[0:cap, :]
    rtag[0:8, :] = stag[0:8, :]

    @pl.loop(1, tiles)
    def _(t):
        pack(t)
        launch(t, 0)

    pos_t[...] = jnp.broadcast_to(pos[0:1, :], (128, rows)).T

    def arrive(t, first):
        for j in range(first, per_tile):
            go_rows(t * per_tile + j).wait_recv()
            go_tags(t * per_tile + j).wait_recv()
        halves = []
        for h in range(TILE // 128):
            tags = rtag[slot_tags(t * per_tile + h * per_lane), :]
            for j in range(1, per_lane):
                tags = tags + rtag[slot_tags(t * per_tile + h * per_lane + j), :]
            halves.append(tags)
        both = jnp.concatenate(halves, axis=1)
        ktag[pl.ds(pl.multiple_of(t * 8, 8), 8), :] = jnp.where(both > 0.0, both, -1.0)
        qtag[tile_of(t), :] = jnp.broadcast_to(both[0:1, :], (128, TILE)).T

    def pair(i, j, fresh=False):
        query, keys = recv[tile_of(i), :], recv[tile_of(j), :]
        sim = lax.dot_general(query, keys, (((1,), (1,)), ((), ())), preferred_element_type=F32)
        left = qtag[tile_of(i), :]
        right = ktag[pl.ds(pl.multiple_of(j * 8, 8), 8), :][0:1, :]
        same = jnp.concatenate([left, left], axis=1) == right
        weight = jnp.where(same, jnp.exp2((sim - 1.0) * SCALE), 0.0)
        dens = weight[:, :128] + weight[:, 128:]
        num = jnp.dot(weight.astype(BF16), keys, preferred_element_type=F32)
        if fresh:
            dacc[tile_of(i), :] = dens
            numer[tile_of(i), :] = num
        else:
            dacc[tile_of(i), :] += dens
            numer[tile_of(i), :] += num

    arrive(0, 1)
    pair(0, 0, True)

    @pl.loop(1, tiles - 1)
    def _(t):
        arrive(t, 0)
        pair(t, t, True)

        @pl.loop(0, t)
        def _(i):
            pair(i, t)
            pair(t, i)

    def finish(t):
        dens = jnp.sum(dacc[tile_of(t), :], axis=1, keepdims=True)
        dens = jnp.where(qtag[tile_of(t), :] > 0.0, dens, 1.0)
        inv = 1.0 / dens
        back[tile_of(t), :] = (
            numer[tile_of(t), :] * jnp.concatenate([inv] * (width // 128), axis=1)).astype(BF16)
        turned = dens.T[0:8, :]
        for j in range(per_tile):
            at = j // per_lane * 128
            bden[slot_tags(t * per_tile + j), :] = own_lanes(turned[:, at:at + 128], j)

    def give(t, first):
        for j in range(first, per_tile):
            back_rows(t * per_tile + j).start()
            back_dens(t * per_tile + j).start()

    last = tiles - 1
    arrive(last, 0)
    pair(last, last, True)
    pair(0, last)
    finish(0)
    give(0, 1)
    home[0:cap, :] = back[0:cap, :]
    hden[0:8, :] = bden[0:8, :]

    @pl.loop(1, last)
    def _(i):
        pair(i, last)
        finish(i)
        give(i, 0)

    @pl.loop(0, last)
    def _(i):
        pair(last, i)

    finish(last)
    give(last, 0)

    def collect(t, first):
        for j in range(first, per_tile):
            back_rows(t * per_tile + j).wait_recv()
            back_dens(t * per_tile + j).wait_recv()
        halves = []
        for h in range(TILE // 128):
            den = hden[slot_tags(t * per_tile + h * per_lane), :]
            for j in range(1, per_lane):
                den = den + hden[slot_tags(t * per_tile + h * per_lane + j), :]
            halves.append(den)
        den = jnp.concatenate(halves, axis=1).astype(BF16)
        den = jnp.dot(den, picks(t), preferred_element_type=F32)
        came = home[tile_of(t), :]
        ids = (lax.broadcasted_iota(jnp.int32, (TILE, TILE), 1) + t * TILE).astype(F32)
        return came, ids, den

    def place(b, came, ids):
        here = pos_t[tile_of(b), :]
        sel = jnp.where(ids == jnp.concatenate([here, here], axis=1), 1.0, 0.0).astype(BF16)
        return jnp.dot(sel, came, preferred_element_type=F32)

    came, ids, den = collect(0, 1)
    out_dens[...] = den
    for b in range(rows // TILE):
        total[tile_of(b), :] = place(b, came, ids)

    @pl.loop(1, last)
    def _(t):
        came, ids, den = collect(t, 0)
        out_dens[...] += den
        for b in range(rows // TILE):
            total[tile_of(b), :] += place(b, came, ids)

    came, ids, den = collect(last, 0)
    out_dens[...] += den
    for b in range(rows // TILE):
        out[tile_of(b), :] = (total[tile_of(b), :] + place(b, came, ids)).astype(BF16)

    @pl.loop(1, n)
    def _(k):
        go_rows(k).wait_send()
        go_tags(k).wait_send()
        back_rows(k).wait_send()
        back_dens(k).wait_send()


def per_device(embeds, labels):
    rows, width = embeds.shape
    n = lax.axis_size("wide")
    slots = 2 * rows
    vmem = pl.BlockSpec(memory_space=pltpu.VMEM)
    average, dens = pl.pallas_call(
        functools.partial(kernel, n),
        out_shape=(jax.ShapeDtypeStruct((rows, width), BF16),
                   jax.ShapeDtypeStruct((8, rows), F32)),
        in_specs=[vmem, vmem],
        out_specs=(vmem, vmem),
        scratch_shapes=[
            pltpu.VMEM((rows, width), BF16),
            pltpu.VMEM((slots, width), BF16),
            pltpu.VMEM((slots, width), BF16),
            pltpu.VMEM((slots, width), BF16),
            pltpu.VMEM((slots, width), BF16),
            pltpu.VMEM((slots, width), F32),
            pltpu.VMEM((rows, width), F32),
            pltpu.VMEM((n * 8, 128), F32),
            pltpu.VMEM((n * 8, 128), F32),
            pltpu.VMEM((n * 8, 128), F32),
            pltpu.VMEM((n * 8, 128), F32),
            pltpu.VMEM((slots // TILE * 8, TILE), F32),
            pltpu.VMEM((slots, 128), F32),
            pltpu.VMEM((slots, 128), F32),
            pltpu.VMEM((8, rows), F32),
            pltpu.VMEM((rows, 128), F32),
        ] + [pltpu.SemaphoreType.DMA((n,))] * 8,
        compiler_params=pltpu.CompilerParams(
            collective_id=0, has_side_effects=True, vmem_limit_bytes=52 * 1024 * 1024),
        cost_estimate=pl.CostEstimate(
            flops=4 * slots * slots * width + 8 * rows * slots * width,
            bytes_accessed=4 * rows * width, transcendentals=slots * slots),
    )(embeds, labels.reshape(1, rows))
    return average, dens[0].astype(BF16)


def solution(mesh):
    placed = (P(("groups", "wide"), None), P(("groups", "wide")))
    return jax.shard_map(
        per_device,
        mesh=mesh,
        in_specs=placed,
        out_specs=(P(("groups", "wide"), None), P(("groups", "wide"))),
        check_vma=False,
    )
```

time: 230 us -> 157 us (0.68)
  the two profiles are of different devices: /device:TPU:15 before, /device:TPU:0 now
where the time goes in v1:
time: 157 us
  Pallas kernels  154 us (98%)
  local copies, waits for them, and re-layouts  2.42 us (2%)
    pallas_call x1, Pallas kernels, per_device(): pl.pallas_call(functools.partial(kernel, n), out_shape=(jax.ShapeDtypeStr...  154 us

profile of v1, /device:TPU:0, one launch (start us, length us, event | category | flops | bytes accessed | tf_op | source)
XLA Modules:
  0.0 157.1 jit_solution(14999659906177252416)
XLA Ops:
  0.6 0.0 copy-start
  0.6 0.7 copy-done
  1.3 154.0 %shard_map.41 = (bf16[1024,768]{1,0:T(8,128)(2,1)S(1)}, f32[8,1024]{1,0:T(8,128)S(1)}) custom-call(bf16[1024,768]{1,0:T(8,128)(2,1)} %embeds.1, s32[1,1024]{1,0:T(1,128)S(1)} %bitcast.1), custom_call_target="tpu_custom_call" | custom-call | flops 25769803776 | bytes 3145728 | tf_op jit(solution)/shard_map/pallas_call | solution.py:265
  155.3 0.6 fusion
  155.9 1.1 copy.5
Async XLA Ops:
  0.6 0.7 copy-start

commit v2 on v1

--- a/solution.py
+++ b/solution.py
@@ -257,7 +257,475 @@
         back_dens(k).wait_send()
 
 
-def per_device(embeds, labels):
+def fast_kernel(n, groups, embeds, labels, out, out_dens, out_flag,
+                unit, send, recv, back, home, numer, total,
+                stag, rtag, bden, hden, ktag, qtag, dacc, pos, pos_t,
+                mtag, tsum, dmat, hsum, otag1, otag2, oden2, oden1, obuf, osum, fin, ssend1, ssend2, flags,
+                s_rows, r_rows, s_tags, r_tags, s_back, r_back, s_den, r_den,
+                s_o1, r_o1, s_o1t, r_o1t, s_o2, r_o2, s_o2t, r_o2t,
+                s_b2, r_b2, s_b2d, r_b2d, s_b1, r_b1, s_b1d, r_b1d, s_f, r_f):
+    rows, width = embeds.shape
+    cap = 2 * rows // n
+    direct = 3 * cap // 4
+    extra = cap // 4
+    layer = 4
+    half = n // 2 * direct
+    gap = n * extra
+    slots = 2 * rows
+    tiles = slots // TILE
+    spare = gap // layer
+    chunks = slots // 128
+    me = lax.axis_index("wide")
+    mine = lax.axis_index("groups") * n + me
+    everyone = groups * n
+    floor, spot = me // layer, lax.rem(me, layer)
+
+    barrier = pltpu.get_barrier_semaphore()
+
+    def nth(q):
+        who = lax.rem(q + everyone, everyone)
+        return {"groups": who // n, "wide": lax.rem(who, n)}
+
+    @pl.loop(1, everyone)
+    def _(q):
+        pl.semaphore_signal(barrier, inc=1, device_id=nth(mine + q), device_id_type=pl.DeviceIdType.MESH)
+
+    def to_dest(k):
+        return {"wide": lax.rem(me + k, n)}
+
+    def to_source(k):
+        return {"wide": lax.rem(me - k + n, n)}
+
+    def across(i):
+        return {"wide": floor * layer + lax.rem(spot + i + layer, layer)}
+
+    def slot_rows(k):
+        return pl.ds(pl.multiple_of(k * direct + k // (n // 2) * gap, 32), direct)
+
+    def eights(k):
+        return pl.ds(pl.multiple_of(k * 8, 8), 8)
+
+    def marks(k):
+        return pl.ds(pl.multiple_of(k * chunks, 8), chunks)
+
+    def tile_of(t):
+        return pl.ds(pl.multiple_of(t * TILE, TILE), TILE)
+
+    def over(i):
+        return pl.ds(half + i * spare, spare)
+
+    def part(j):
+        return pl.ds(half + j * extra, extra)
+
+    def remote(src, dst, ssem, rsem, where):
+        return pltpu.make_async_remote_copy(
+            src_ref=src, dst_ref=dst, send_sem=ssem, recv_sem=rsem,
+            device_id=where, device_id_type=pl.DeviceIdType.MESH)
+
+    def go_rows(k):
+        return remote(send.at[slot_rows(k)], recv.at[slot_rows(k)], s_rows.at[k], r_rows.at[k], to_dest(k))
+
+    def go_tags(k):
+        return remote(stag.at[marks(k)], rtag.at[marks(k)], s_tags.at[k], r_tags.at[k], to_dest(k))
+
+    def back_rows(k):
+        return remote(back.at[slot_rows(k)], home.at[slot_rows(k)], s_back.at[k], r_back.at[k], to_source(k))
+
+    def back_dens(k):
+        return remote(bden.at[marks(k)], hden.at[marks(k)], s_den.at[k], r_den.at[k], to_source(k))
+
+    def one_rows(j):
+        return remote(send.at[part(0)], recv.at[part(j)], s_o1.at[j], r_o1.at[j], to_dest(layer * j))
+
+    def one_tags(j):
+        return remote(ssend1.at[eights(j)], otag1.at[eights(j)], s_o1t.at[j], r_o1t.at[j], to_dest(layer * j))
+
+    def two_rows(i):
+        return remote(recv.at[over(0)], recv.at[over(i)], s_o2.at[i], r_o2.at[i], across(i))
+
+    def two_tags(i):
+        return remote(otag2.at[eights(0)], otag2.at[eights(i)], s_o2t.at[i], r_o2t.at[i], across(i))
+
+    def three_rows(i):
+        return remote(back.at[over(i)], obuf.at[pl.ds(i * spare, spare)], s_b2.at[i], r_b2.at[i], across(-i))
+
+    def three_dens(i):
+        return remote(ssend2.at[eights(i)], oden2.at[eights(i)], s_b2d.at[i], r_b2d.at[i], across(-i))
+
+    def four_rows(j):
+        return remote(osum.at[pl.ds(j * extra, extra)], fin.at[pl.ds(j * extra, extra)],
+                      s_b1.at[j], r_b1.at[j], to_source(layer * j))
+
+    def four_dens(j):
+        return remote(ssend1.at[eights(layer + j)], oden1.at[eights(j)], s_b1d.at[j], r_b1d.at[j],
+                      to_source(layer * j))
+
+    def tell(q):
+        return remote(flags.at[eights(0)], flags.at[eights(q)], s_f.at[q], r_f.at[q], nth(mine + q))
+
+    @pl.loop(0, rows // 128)
+    def _(b):
+        at = pl.ds(pl.multiple_of(b * 128, 128), 128)
+        x = embeds[at, :].astype(F32)
+        inside = jnp.sum(x * x, axis=1, keepdims=True) + 1e-06
+        unit[at, :] = (x * lax.rsqrt(inside)).astype(BF16)
+
+    lab = labels[...]
+    ahead = (lab >> 2) - me
+    ahead = jnp.where(ahead < 0, ahead + n, ahead)
+    which = lax.broadcasted_iota(jnp.int32, (n, TILE), 0)
+    before = (lax.broadcasted_iota(jnp.int32, (TILE, TILE), 0)
+              < lax.broadcasted_iota(jnp.int32, (TILE, TILE), 1)).astype(F32).astype(BF16)
+    running = jnp.zeros((n, 1), F32)
+    beyond = jnp.zeros((8, 1), F32)
+    for b in range(rows // TILE):
+        piece = ahead[:, b * TILE:(b + 1) * TILE]
+        hot = (jnp.broadcast_to(piece, (n, TILE)) == which).astype(F32)
+        rank = jnp.dot(hot.astype(BF16), before, preferred_element_type=F32) + running
+        running = running + jnp.sum(hot, axis=1, keepdims=True)
+        rank = jnp.broadcast_to(jnp.sum(hot * rank, axis=0, keepdims=True), (8, TILE))
+        base = jnp.broadcast_to(
+            (piece * direct + jnp.where(piece >= n // 2, gap, 0)).astype(F32), (8, TILE))
+        past = jnp.where(rank >= direct, 1.0, 0.0)
+        late = jnp.dot(past.astype(BF16), before, preferred_element_type=F32) + beyond
+        beyond = beyond + jnp.sum(past, axis=1, keepdims=True)
+        spill = jnp.where(late < extra, late + half, -1.0)
+        pos[:, b * TILE:(b + 1) * TILE] = jnp.where(past > 0.0, spill, base + rank)
+    flags[eights(0), :] = jnp.broadcast_to(jnp.where(beyond > extra, 1.0, 0.0), (8, 128))
+
+    tag8 = jnp.broadcast_to(((lab & 3) + 1).astype(F32), (8, rows)).astype(BF16)
+    full8 = jnp.broadcast_to((lab + 1).astype(F32), (8, rows)).astype(BF16)
+    lane = lax.broadcasted_iota(jnp.int32, (8, 128), 1)
+    index = (lax.broadcasted_iota(jnp.int32, (chunks, 128), 0) * 128
+             + lax.broadcasted_iota(jnp.int32, (chunks, 128), 1))
+    contract = (((1,), (1,)), ((), ()))
+
+    def picks(t, count=TILE):
+        ids = (lax.broadcasted_iota(jnp.int32, (count, rows), 0) + t * TILE).astype(F32)
+        return jnp.where(ids == pos[0:1, :], 1.0, 0.0).astype(BF16)
+
+    def own(matrix, k):
+        low = k * direct + k // (n // 2) * gap
+        return jnp.where((index >= low) & (index < low + direct), matrix, 0.0)
+
+    def lanes(piece, j):
+        return jnp.where((lane >= j * extra) & (lane < (j + 1) * extra), piece, 0.0)
+
+    over_tile = half // TILE
+    sel = picks(over_tile, 128)
+    send[half:half + 128, :] = jnp.dot(sel, unit[...], preferred_element_type=F32).astype(BF16)
+    labels0 = lax.dot_general(full8, sel, contract, preferred_element_type=F32)
+    labels0 = lanes(labels0, 0)
+    otag1[0:8, :] = labels0
+    for j in range(1, layer):
+        ssend1[j * 8:j * 8 + 8, :] = pltpu.roll(labels0, j * extra, 1)
+    recv[half:half + extra, :] = send[half:half + extra, :]
+    pl.semaphore_wait(barrier, everyone - 1)
+    for j in range(1, layer):
+        one_rows(j).start()
+        one_tags(j).start()
+
+    @pl.loop(1, everyone)
+    def _(q):
+        tell(q).start()
+
+    mtag[...] = jnp.zeros_like(mtag)
+
+    def pack(t):
+        sel = picks(t)
+        send[tile_of(t), :] = jnp.dot(sel, unit[...], preferred_element_type=F32).astype(BF16)
+        tags = lax.dot_general(tag8, sel, contract, preferred_element_type=F32)
+        mtag[2 * t:2 * t + 1, :] = tags[0:1, :128]
+        mtag[2 * t + 1:2 * t + 2, :] = tags[0:1, 128:]
+
+    low_tiles = half // TILE
+    packed = list(range(low_tiles)) + list(range(tiles - low_tiles, tiles))
+
+    def start_of(k):
+        return k * direct + k // (n // 2) * gap
+
+    ready = 0
+    for t in packed:
+        pack(t)
+        if t == 0:
+            recv[0:direct, :] = send[0:direct, :]
+        while ready < n and start_of(ready) + direct <= (t + 1) * TILE:
+            if ready > 0:
+                go_rows(ready).start()
+            ready += 1
+
+    every = mtag[...]
+    tsum[...] = own(every, 0)
+
+    @pl.loop(1, n)
+    def _(k):
+        stag[marks(k), :] = own(every, k)
+        go_tags(k).start()
+
+    for j in range(1, layer):
+        one_rows(j).wait_recv()
+        one_tags(j).wait_recv()
+    otag2[0:8, :] = otag1[0:8, :] + otag1[8:16, :] + otag1[16:24, :] + otag1[24:32, :]
+    for i in range(1, layer):
+        two_rows(i).start()
+        two_tags(i).start()
+
+    pos_t[...] = jnp.broadcast_to(pos[0:1, :], (128, rows)).T
+
+    def note(t, both):
+        both = jnp.broadcast_to(both, (8, TILE))
+        ktag[t * 8:t * 8 + 8, :] = jnp.where(both > 0.0, both, -1.0)
+        qtag[t * TILE:(t + 1) * TILE, :] = jnp.broadcast_to(both[0:1, :], (128, TILE)).T
+
+    def ends(t):
+        if t < low_tiles:
+            first, last = t * TILE, (t + 1) * TILE
+        else:
+            first, last = t * TILE, (t + 1) * TILE
+        return [k for k in range(1, n) if first <= start_of(k) < last]
+
+    def arrive(t):
+        if low_tiles <= t < tiles - low_tiles:
+            chosen = []
+            for i in (2 * (t - low_tiles), 2 * (t - low_tiles) + 1):
+                if i > 0:
+                    two_rows(i).wait_recv()
+                    two_tags(i).wait_recv()
+                value = otag2[i * 8:i * 8 + 1, :] - (me * CL_DEV).astype(F32)
+                chosen.append(jnp.where((value > 0.5) & (value < CL_DEV + 0.5), value, 0.0))
+            note(t, jnp.concatenate(chosen, axis=1))
+            return
+        for k in ends(t):
+            go_rows(k).wait_recv()
+            go_tags(k).wait_recv()
+            tsum[...] += rtag[marks(k), :]
+        note(t, jnp.concatenate([tsum[2 * t:2 * t + 1, :], tsum[2 * t + 1:2 * t + 2, :]], axis=1))
+
+    def pair(i, j, fresh=False):
+        query, keys = recv[tile_of(i), :], recv[tile_of(j), :]
+        sim = lax.dot_general(query, keys, contract, preferred_element_type=F32)
+        left = qtag[tile_of(i), :]
+        right = ktag[eights(j), :][0:1, :]
+        same = jnp.concatenate([left, left], axis=1) == right
+        weight = jnp.where(same, jnp.exp2((sim - 1.0) * SCALE), 0.0)
+        dens = weight[:, :128] + weight[:, 128:]
+        num = jnp.dot(weight.astype(BF16), keys, preferred_element_type=F32)
+        if fresh:
+            dacc[tile_of(i), :] = dens
+            numer[tile_of(i), :] = num
+        else:
+            dacc[tile_of(i), :] += dens
+            numer[tile_of(i), :] += num
+
+    last = tiles - 1
+    arrive(0)
+    pair(0, 0, True)
+
+    @pl.loop(1, last)
+    def _(t):
+        for at in range(1, last):
+            @pl.when(t == at)
+            def _():
+                arrive(at)
+        pair(t, t, True)
+
+        @pl.loop(0, t)
+        def _(i):
+            pair(i, t)
+            pair(t, i)
+
+    def finish(t):
+        dens = jnp.sum(dacc[tile_of(t), :], axis=1, keepdims=True)
+        live = qtag[tile_of(t), :] > 0.0
+        inv = 1.0 / jnp.where(live, dens, 1.0)
+        back[tile_of(t), :] = (
+            numer[tile_of(t), :] * jnp.concatenate([inv] * (width // 128), axis=1)).astype(BF16)
+        turned = jnp.where(live, dens, 0.0).T
+        dmat[pl.ds(2 * t, 1), :] = turned[0:1, :128]
+        dmat[pl.ds(2 * t + 1, 1), :] = turned[0:1, 128:]
+
+    arrive(last)
+    pair(last, last, True)
+
+    @pl.loop(low_tiles, tiles - low_tiles)
+    def _(i):
+        pair(i, last)
+        finish(i)
+
+    for i in range(1, layer):
+        row = half // 128 + i
+        ssend2[i * 8:i * 8 + 8, :] = jnp.broadcast_to(dmat[row:row + 1, :], (8, 128))
+        three_rows(i).start()
+        three_dens(i).start()
+
+    sent = 0
+    for t in packed[:-1]:
+        pair(t, last)
+        finish(t)
+        if t == 0:
+            home[0:direct, :] = back[0:direct, :]
+        while sent < n and start_of(sent) + direct <= (t + 1) * TILE:
+            if sent > 0:
+                back_rows(sent).start()
+            sent += 1
+
+    summed = back[half:half + spare, :].astype(F32)
+    here = half // 128
+    dens_over = jnp.broadcast_to(dmat[here:here + 1, :], (8, 128))
+    for i in range(1, layer):
+        three_rows(i).wait_recv()
+        three_dens(i).wait_recv()
+        summed = summed + obuf[i * spare:(i + 1) * spare, :].astype(F32)
+        dens_over = dens_over + oden2[i * 8:i * 8 + 8, :]
+    osum[...] = summed.astype(BF16)
+    for j in range(1, layer):
+        ssend1[(layer + j) * 8:(layer + j) * 8 + 8, :] = pltpu.roll(
+            lanes(dens_over, j), 128 - j * extra, 1)
+        four_rows(j).start()
+        four_dens(j).start()
+
+    @pl.loop(0, last)
+    def _(i):
+        pair(last, i)
+
+    finish(last)
+    for k in range(sent, n):
+        back_rows(k).start()
+
+    every_den = dmat[...]
+    hsum[...] = own(every_den, 0)
+
+    @pl.loop(1, n)
+    def _(k):
+        bden[marks(k), :] = own(every_den, k)
+        back_dens(k).start()
+
+    home[half + extra:half + gap, :] = jnp.zeros((gap - extra, width), BF16)
+
+    def place(b, t):
+        here = pos_t[tile_of(b), :]
+        ids = (lax.broadcasted_iota(jnp.int32, (TILE, TILE), 1) + t * TILE).astype(F32)
+        sel = jnp.where(ids == jnp.concatenate([here, here], axis=1), 1.0, 0.0).astype(BF16)
+        return jnp.dot(sel, home[tile_of(t), :], preferred_element_type=F32)
+
+    def collect(t):
+        for k in ends(t):
+            back_rows(k).wait_recv()
+
+    collect(0)
+
+    @pl.loop(0, rows // TILE)
+    def _(b):
+        total[tile_of(b), :] = place(b, 0)
+
+    for t in packed[1:low_tiles]:
+        collect(t)
+
+        @pl.loop(0, rows // TILE)
+        def _(b):
+            total[tile_of(b), :] += place(b, t)
+
+    for j in range(1, layer):
+        four_rows(j).wait_recv()
+        four_dens(j).wait_recv()
+    mine_over = osum[0:extra, :].astype(F32)
+    den_over = lanes(dens_over, 0)
+    for j in range(1, layer):
+        mine_over = mine_over + fin[j * extra:(j + 1) * extra, :].astype(F32)
+        den_over = den_over + oden1[j * 8:j * 8 + 8, :]
+    home[half:half + extra, :] = mine_over.astype(BF16)
+
+    for t in [over_tile] + packed[low_tiles:-1]:
+        if t != over_tile:
+            collect(t)
+
+        @pl.loop(0, rows // TILE)
+        def _(b):
+            total[tile_of(b), :] += place(b, t)
+
+    @pl.loop(1, n)
+    def _(k):
+        back_dens(k).wait_recv()
+        hsum[...] += hden[marks(k), :]
+
+    hsum[here:here + 1, :] = den_over[0:1, :]
+
+    den = jnp.zeros((8, rows), F32)
+    for t in packed[:low_tiles] + [over_tile] + packed[low_tiles:]:
+        row = jnp.concatenate([hsum[2 * t:2 * t + 1, :], hsum[2 * t + 1:2 * t + 2, :]], axis=1)
+        row = jnp.broadcast_to(row, (8, TILE)).astype(BF16)
+        den = den + jnp.dot(row, picks(t), preferred_element_type=F32)
+    out_dens[...] = den
+
+    collect(last)
+
+    @pl.loop(0, rows // TILE)
+    def _(b):
+        out[tile_of(b), :] = (total[tile_of(b), :] + place(b, last)).astype(BF16)
+
+    out_flag[...] = flags[eights(0), :]
+
+    @pl.loop(1, everyone)
+    def _(q):
+        tell(q).wait()
+        out_flag[...] = jnp.maximum(out_flag[...], flags[eights(q), :])
+
+    for j in range(1, layer):
+        for copy in (one_rows(j), one_tags(j), two_rows(j), two_tags(j),
+                     three_rows(j), three_dens(j), four_rows(j), four_dens(j)):
+            copy.wait_send()
+
+    @pl.loop(1, n)
+    def _(k):
+        go_rows(k).wait_send()
+        go_tags(k).wait_send()
+        back_rows(k).wait_send()
+        back_dens(k).wait_send()
+
+
+def fast(embeds, labels):
+    rows, width = embeds.shape
+    n, groups = lax.axis_size("wide"), lax.axis_size("groups")
+    slots = 2 * rows
+    chunks = slots // 128
+    cap = slots // n
+    vmem = pl.BlockSpec(memory_space=pltpu.VMEM)
+
+    def tall(count):
+        return pltpu.VMEM((count, 128), F32)
+
+    def wide(count, kind=BF16):
+        return pltpu.VMEM((count, width), kind)
+
+    sems = [pltpu.SemaphoreType.DMA((n,))] * 8 + [pltpu.SemaphoreType.DMA((4,))] * 16
+    sems = sems + [pltpu.SemaphoreType.DMA((groups * n,))] * 2
+    return pl.pallas_call(
+        functools.partial(fast_kernel, n, groups),
+        out_shape=(jax.ShapeDtypeStruct((rows, width), BF16),
+                   jax.ShapeDtypeStruct((8, rows), F32),
+                   jax.ShapeDtypeStruct((8, 128), F32)),
+        in_specs=[vmem, vmem],
+        out_specs=(vmem, vmem, vmem),
+        scratch_shapes=[
+            wide(rows), wide(slots), wide(slots), wide(slots), wide(slots),
+            wide(slots, F32), wide(rows, F32),
+            tall(n * chunks), tall(n * chunks), tall(n * chunks), tall(n * chunks),
+            pltpu.VMEM((slots // TILE * 8, TILE), F32),
+            tall(slots), tall(slots),
+            pltpu.VMEM((8, rows), F32), tall(rows),
+            tall(chunks), tall(chunks), tall(chunks), tall(chunks),
+            tall(32), tall(32), tall(32), tall(32),
+            wide(cap * 4), wide(cap), wide(cap), tall(64), tall(32), tall(groups * n * 8),
+        ] + sems,
+        compiler_params=pltpu.CompilerParams(
+            collective_id=1, has_side_effects=True, vmem_limit_bytes=52 * 1024 * 1024),
+        cost_estimate=pl.CostEstimate(
+            flops=4 * slots * slots * width + 8 * rows * slots * width,
+            bytes_accessed=4 * rows * width, transcendentals=slots * slots),
+    )(embeds, labels)
+
+
+def plain(embeds, labels):
     rows, width = embeds.shape
     n = lax.axis_size("wide")
     slots = 2 * rows
@@ -291,7 +759,19 @@
         cost_estimate=pl.CostEstimate(
             flops=4 * slots * slots * width + 8 * rows * slots * width,
             bytes_accessed=4 * rows * width, transcendentals=slots * slots),
-    )(embeds, labels.reshape(1, rows))
+    )(embeds, labels)
+    return average, dens
+
+
+def per_device(embeds, labels):
+    rows = embeds.shape[0]
+    line = labels.reshape(1, rows)
+    if lax.axis_size("wide") == 16 and 2 * rows // 16 == 128:
+        average, dens, flag = fast(embeds, line)
+        average, dens = lax.cond(
+            flag[0, 0] > 0.0, lambda: tuple(plain(embeds, line)), lambda: (average, dens))
+    else:
+        average, dens = plain(embeds, line)
     return average, dens[0].astype(BF16)
 
 

time: 157 us -> 172 us (1.096)
  Pallas kernels: 154 us -> 169 us
    pallas_call x1, Pallas kernels: 154 us -> 169 us  [fast(): pl.pallas_call(functools.partial(fast_kernel, n, groups), out_shape=(jax....]
where the time goes in v2:
time: 172 us
  Pallas kernels  169 us (98%)
  local copies, waits for them, and re-layouts  2.26 us (1%)
    pallas_call x1, Pallas kernels, fast(): pl.pallas_call(functools.partial(fast_kernel, n, groups), out_shape=(jax....  169 us

profile of v2, /device:TPU:0, one launch (start us, length us, event | category | flops | bytes accessed | tf_op | source)
XLA Modules:
  0.0 172.3 jit_solution(2248586898883369778)
XLA Ops:
  0.6 0.0 copy-start
  0.6 0.0 copy-start.1
  0.6 168.5 %shard_map.41 = (bf16[1024,768]{1,0:T(8,128)(2,1)S(1)}, f32[8,1024]{1,0:T(8,128)S(1)}, f32[8,128]{1,0:T(8,128)S(1)}) custom-call(bf16[1024,768]{1,0:T(8,128)(2,1)} %embeds.1, s32[1,1024]{1,0:T(1,128)} %bitcast.2), custom_call_target="tpu_custom_call" | custom-call | flops 25769803776 | bytes 3145728 | tf_op jit(solution)/shard_map/pallas_call | solution.py:702
  169.2 0.5 slice.15
  170.3 0.0 copy-done
  170.3 0.0 copy-done.1
  170.3 0.2 conditional.2
  170.5 0.6 fusion
  171.1 1.1 copy.9
Async XLA Ops:
  0.6 169.7 %copy-start = (bf16[1024,768]{1,0:T(8,128)(2,1)S(1)}, bf16[1024,768]{1,0:T(8,128)(2,1)}, u32[]{:S(2)}) copy-start(bf16[1024,768]{1,0:T(8,128)(2,1)} %embeds.1) | copy-start | bytes 4718596
  0.6 169.7 %copy-start.1 = (s32[1024]{0:T(1024)S(1)}, s32[1024]{0:T(1024)}, u32[]{:S(2)}) copy-start(s32[1024]{0:T(1024)} %param.5) | copy-start | bytes 12292

commit v3 on v2

--- a/solution.py
+++ b/solution.py
@@ -259,7 +259,7 @@
 
 def fast_kernel(n, groups, embeds, labels, out, out_dens, out_flag,
                 unit, send, recv, back, home, numer, total,
-                stag, rtag, bden, hden, ktag, qtag, dacc, pos, pos_t,
+                stag, rtag, bden, hden, ktag, qtag, dacc, drow, pos, pos_t,
                 mtag, tsum, dmat, hsum, otag1, otag2, oden2, oden1, obuf, osum, fin, ssend1, ssend2, flags,
                 s_rows, r_rows, s_tags, r_tags, s_back, r_back, s_den, r_den,
                 s_o1, r_o1, s_o1t, r_o1t, s_o2, r_o2, s_o2t, r_o2t,
@@ -451,24 +451,20 @@
             recv[0:direct, :] = send[0:direct, :]
         while ready < n and start_of(ready) + direct <= (t + 1) * TILE:
             if ready > 0:
+                stag[ready * chunks:(ready + 1) * chunks, :] = own(mtag[...], ready)
+                go_tags(ready).start()
                 go_rows(ready).start()
             ready += 1
-
-    every = mtag[...]
-    tsum[...] = own(every, 0)
-
-    @pl.loop(1, n)
-    def _(k):
-        stag[marks(k), :] = own(every, k)
-        go_tags(k).start()
-
-    for j in range(1, layer):
-        one_rows(j).wait_recv()
-        one_tags(j).wait_recv()
-    otag2[0:8, :] = otag1[0:8, :] + otag1[8:16, :] + otag1[16:24, :] + otag1[24:32, :]
-    for i in range(1, layer):
-        two_rows(i).start()
-        two_tags(i).start()
+        if t == low_tiles - 1:
+            for j in range(1, layer):
+                one_rows(j).wait_recv()
+                one_tags(j).wait_recv()
+            otag2[0:8, :] = otag1[0:8, :] + otag1[8:16, :] + otag1[16:24, :] + otag1[24:32, :]
+            for i in range(1, layer):
+                two_rows(i).start()
+                two_tags(i).start()
+
+    tsum[...] = own(mtag[...], 0)
 
     pos_t[...] = jnp.broadcast_to(pos[0:1, :], (128, rows)).T
 
@@ -517,6 +513,23 @@
             dacc[tile_of(i), :] += dens
             numer[tile_of(i), :] += num
 
+    def both(i, t):
+        query, keys = recv[tile_of(i), :], recv[tile_of(t), :]
+        sim = lax.dot_general(query, keys, contract, preferred_element_type=F32)
+        left = qtag[tile_of(i), :]
+        right = ktag[eights(t), :][0:1, :]
+        same = jnp.concatenate([left, left], axis=1) == right
+        weight = jnp.where(same, jnp.exp2((sim - 1.0) * SCALE), 0.0)
+        rounded = weight.astype(BF16)
+        num_i = jnp.dot(rounded, keys, preferred_element_type=F32)
+        num_t = lax.dot_general(rounded, query, (((0,), (0,)), ((), ())), preferred_element_type=F32)
+        old_i, old_t = numer[tile_of(i), :], numer[tile_of(t), :]
+        dacc[tile_of(i), :] += weight[:, :128] + weight[:, 128:]
+        drow[eights(t), :] += jnp.sum(weight.reshape(TILE // 8, 8, TILE), axis=0)
+        numer[tile_of(i), :] = old_i + num_i
+        numer[tile_of(t), :] = old_t + num_t
+
+    drow[...] = jnp.zeros_like(drow)
     last = tiles - 1
     arrive(0)
     pair(0, 0, True)
@@ -531,11 +544,12 @@
 
         @pl.loop(0, t)
         def _(i):
-            pair(i, t)
-            pair(t, i)
+            both(i, t)
 
     def finish(t):
-        dens = jnp.sum(dacc[tile_of(t), :], axis=1, keepdims=True)
+        down = jnp.sum(drow[eights(t), :], axis=0, keepdims=True)
+        dens = (jnp.sum(dacc[tile_of(t), :], axis=1, keepdims=True)
+                + jnp.broadcast_to(down, (128, TILE)).T)
         live = qtag[tile_of(t), :] > 0.0
         inv = 1.0 / jnp.where(live, dens, 1.0)
         back[tile_of(t), :] = (
@@ -549,7 +563,7 @@
 
     @pl.loop(low_tiles, tiles - low_tiles)
     def _(i):
-        pair(i, last)
+        both(i, last)
         finish(i)
 
     for i in range(1, layer):
@@ -560,7 +574,7 @@
 
     sent = 0
     for t in packed[:-1]:
-        pair(t, last)
+        both(t, last)
         finish(t)
         if t == 0:
             home[0:direct, :] = back[0:direct, :]
@@ -584,10 +598,6 @@
         four_rows(j).start()
         four_dens(j).start()
 
-    @pl.loop(0, last)
-    def _(i):
-        pair(last, i)
-
     finish(last)
     for k in range(sent, n):
         back_rows(k).start()
@@ -614,15 +624,13 @@
 
     collect(0)
 
-    @pl.loop(0, rows // TILE)
-    def _(b):
+    for b in range(rows // TILE):
         total[tile_of(b), :] = place(b, 0)
 
     for t in packed[1:low_tiles]:
         collect(t)
 
-        @pl.loop(0, rows // TILE)
-        def _(b):
+        for b in range(rows // TILE):
             total[tile_of(b), :] += place(b, t)
 
     for j in range(1, layer):
@@ -639,8 +647,7 @@
         if t != over_tile:
             collect(t)
 
-        @pl.loop(0, rows // TILE)
-        def _(b):
+        for b in range(rows // TILE):
             total[tile_of(b), :] += place(b, t)
 
     @pl.loop(1, n)
@@ -659,8 +666,7 @@
 
     collect(last)
 
-    @pl.loop(0, rows // TILE)
-    def _(b):
+    for b in range(rows // TILE):
         out[tile_of(b), :] = (total[tile_of(b), :] + place(b, last)).astype(BF16)
 
     out_flag[...] = flags[eights(0), :]
@@ -711,7 +717,7 @@
             wide(slots, F32), wide(rows, F32),
             tall(n * chunks), tall(n * chunks), tall(n * chunks), tall(n * chunks),
             pltpu.VMEM((slots // TILE * 8, TILE), F32),
-            tall(slots), tall(slots),
+            tall(slots), tall(slots), pltpu.VMEM((slots // TILE * 8, TILE), F32),
             pltpu.VMEM((8, rows), F32), tall(rows),
             tall(chunks), tall(chunks), tall(chunks), tall(chunks),
             tall(32), tall(32), tall(32), tall(32),

time: 172 us -> 146 us (0.85)
  Pallas kernels: 169 us -> 143 us
    pallas_call x1, Pallas kernels: 169 us -> 143 us  [fast(): pl.pallas_call(functools.partial(fast_kernel, n, groups), out_shape=(jax....]
where the time goes in v3:
time: 146 us
  Pallas kernels  143 us (98%)
  local copies, waits for them, and re-layouts  2.26 us (2%)
    pallas_call x1, Pallas kernels, fast(): pl.pallas_call(functools.partial(fast_kernel, n, groups), out_shape=(jax....  143 us

profile of v3, /device:TPU:0, one launch (start us, length us, event | category | flops | bytes accessed | tf_op | source)
XLA Modules:
  0.0 146.1 jit_solution(15894975078972204658)
XLA Ops:
  0.6 0.0 copy-start
  0.6 0.0 copy-start.1
  0.6 142.5 %shard_map.41 = (bf16[1024,768]{1,0:T(8,128)(2,1)S(1)}, f32[8,1024]{1,0:T(8,128)S(1)}, f32[8,128]{1,0:T(8,128)S(1)}) custom-call(bf16[1024,768]{1,0:T(8,128)(2,1)} %embeds.1, s32[1,1024]{1,0:T(1,128)} %bitcast.2), custom_call_target="tpu_custom_call" | custom-call | flops 25769803776 | bytes 3145728 | tf_op jit(solution)/shard_map/pallas_call | solution.py:708
  143.2 0.5 slice.15
  144.3 0.0 copy-done
  144.3 0.0 copy-done.1
  144.4 0.6 fusion
  145.0 1.1 copy.9
  (1 shorter events, 0.0 us)
Async XLA Ops:
  0.6 143.7 %copy-start = (bf16[1024,768]{1,0:T(8,128)(2,1)S(1)}, bf16[1024,768]{1,0:T(8,128)(2,1)}, u32[]{:S(2)}) copy-start(bf16[1024,768]{1,0:T(8,128)(2,1)} %embeds.1) | copy-start | bytes 4718596
  0.6 143.7 %copy-start.1 = (s32[1024]{0:T(1024)S(1)}, s32[1024]{0:T(1024)}, u32[]{:S(2)}) copy-start(s32[1024]{0:T(1024)} %param.5) | copy-start | bytes 12292
